TPU v7x, 32 devices: a whole 2x2x4 slice. The times are simulated.
32 devices in a mesh: groups: 2 (over y), seq: 4 (over z), heads: 2 (over x), users: 2 (over core).
Axes of the slice: x: 2, y: 2, z: 4, core: 2. Of those that a mesh axis runs over, the one named last changes fastest.
Arguments:
- queries: bfloat16 [16, 256, 512], P(('groups', 'users'), 'seq', 'heads'), parts along dimension 0, may hold values from -8 to 8
- keys: bfloat16 [16, 8192, 512], P(('groups', 'users'), 'seq', 'heads'), parts along dimension 0, may hold values from -8 to 8
- values: bfloat16 [16, 8192, 512], P(('groups', 'users'), 'seq', 'heads'), parts along dimension 0, may hold values from -16 to 16
- hist_len: int32 [16], P(('groups', 'users')), parts along dimension 0, may hold values from 1 to 8192, as said below
- block_ids: int32 [16, 256, 4, 8], P(('groups', 'users'), None, 'seq'), parts along dimension 0, may hold values from 0 to 15, as said below
- block_count: int32 [16, 256, 4], P(('groups', 'users'), None, 'seq'), parts along dimension 0, may hold values from 0 to 8, as said below
- out_weight: bfloat16 [512, 512], P('heads'), may hold values from -0.75 to 0.75
Outputs:
- joined: bfloat16 [16, 256, 512], P(('groups', 'users'), 'seq', 'heads'), parts along dimension 0
There are 2 independent parts, one for each index of `groups`. A program takes and returns all parts, laid end to end along the dimension named above; an argument that names none is the same for every part. Nothing has to cross between parts.
Inputs may be any that keep to these rules, and one draw needn't show every extreme that they name: `block_ids`: the first block_count entries of a candidate's list for a shard are distinct blocks of that shard holding at least one event of the user's history; the remaining entries are unused. `block_count`: at least 1 on the first shard for every candidate; 0 exactly on shards holding none of the user's history; equal to 8 for some candidate. `hist_len`: some user's history fills all 8192 events.
All inputs are finite; a program needn't handle non-finite values.
Results may differ from a plain program's by a relative error of at most 0.011.
Values may be sent and summed in bfloat16 or wider, within the bound.
A program may use at most 64 MiB of HBM per device.

v0:
```python
import jax
import jax.numpy as jnp
from jax import lax
from jax.sharding import PartitionSpec as P

HD = 64
BLOCK = 128


def passed_along(value, axis, steps):
    count = lax.axis_size(axis)
    pairs = [(source, (source + steps) % count) for source in range(count)]
    return lax.ppermute(value, axis, pairs)


def shard_mask(id_rows, count_rows, length, shard_index, events):
    blocks = jnp.arange(events // BLOCK, dtype=jnp.int32)
    slot_range = jnp.arange(id_rows.shape[1], dtype=jnp.int32)
    matches = (id_rows[:, :, None] == blocks[None, None, :]) & (
        slot_range[None, :, None] < count_rows[:, None, None]
    )
    chosen = jnp.any(matches, axis=1)
    event_chosen = jnp.repeat(chosen, BLOCK, axis=1)
    position = shard_index * events + jnp.arange(events, dtype=jnp.int32)
    return event_chosen & (position < length)[None, :]


def combine(first, second):
    peak_score = jnp.maximum(first[0], second[0])
    scale_first = jnp.exp(first[0] - peak_score)
    scale_second = jnp.exp(second[0] - peak_score)
    weight_sum = first[1] * scale_first + second[1] * scale_second
    weighted = first[2] * jnp.repeat(scale_first, HD, axis=-1) + second[2] * jnp.repeat(
        scale_second, HD, axis=-1
    )
    return (peak_score, weight_sum, weighted)


def body(queries, keys, values, hist_len, block_ids, block_count, out_weight):
    user_count = queries.shape[0]
    visit_rows = queries.shape[1]
    feature_width = queries.shape[2]
    local_heads = feature_width // HD
    events = keys.shape[1]
    seq_size = lax.axis_size("seq")
    seq_place = lax.axis_index("seq")
    key_heads = keys.reshape(user_count, events, local_heads, HD)
    value_heads = values.reshape(user_count, events, local_heads, HD)
    ids_here = block_ids[:, :, 0, :]
    counts_here = block_count[:, :, 0]
    score_scale = HD ** (-0.5)

    def local_part(query_block, id_block, count_block):

        def per_user(inputs):
            query_user, key_user, value_user, length, id_rows, count_rows = inputs
            row_count = query_user.shape[0]
            selected = shard_mask(id_rows, count_rows, length, seq_place, events)
            query_split = query_user.reshape(row_count, local_heads, HD)
            scores = (
                jnp.einsum(
                    "rhd,ehd->rhe", query_split, key_user, preferred_element_type=jnp.float32
                )
                * score_scale
            )
            scores = jnp.where(selected[:, None, :], scores, -1e30)
            peak_score = jnp.max(scores, axis=2)
            weight = jnp.where(selected[:, None, :], jnp.exp(scores - peak_score[:, :, None]), 0.0)
            weight_sum = jnp.sum(weight, axis=2)
            weighted = jnp.einsum(
                "rhe,ehd->rhd",
                weight.astype(jnp.bfloat16),
                value_user,
                preferred_element_type=jnp.float32,
            )
            return (peak_score, weight_sum, weighted.reshape(row_count, feature_width))

        return lax.map(
            per_user, (query_block, key_heads, value_heads, hist_len, id_block, count_block)
        )

    def tour_step(step_index, running):
        travel_query, peak_score, weight_sum, weighted = running
        anchor = (seq_place - step_index) % seq_size
        first_row = anchor * visit_rows
        id_block = lax.dynamic_slice_in_dim(ids_here, first_row, visit_rows, 1)
        count_block = lax.dynamic_slice_in_dim(counts_here, first_row, visit_rows, 1)
        partial_value = local_part(travel_query, id_block, count_block)
        peak_score, weight_sum, weighted = combine(
            (peak_score, weight_sum, weighted), partial_value
        )
        travel_query = passed_along(travel_query, "seq", 1)
        peak_score, weight_sum, weighted = passed_along(
            (peak_score, weight_sum, weighted), "seq", 1
        )
        return (travel_query, peak_score, weight_sum, weighted)

    def two_steps(half_index, running):
        running = tour_step(2 * half_index, running)
        return tour_step(2 * half_index + 1, running)

    start = (
        queries,
        jnp.full((user_count, visit_rows, local_heads), -1e30, jnp.float32),
        jnp.zeros((user_count, visit_rows, local_heads), jnp.float32),
        jnp.zeros((user_count, visit_rows, feature_width), jnp.float32),
    )
    _, peak_score, weight_sum, weighted = lax.fori_loop(0, seq_size // 2, two_steps, start)
    attended = (weighted / jnp.repeat(weight_sum, HD, axis=2)).astype(jnp.bfloat16)
    projected = jnp.einsum("urw,wd->urd", attended, out_weight, preferred_element_type=jnp.float32)
    joined = lax.psum_scatter(
        projected.astype(jnp.bfloat16), "heads", scatter_dimension=2, tiled=True
    )
    return joined


def solution(mesh):
    return jax.shard_map(
        body,
        mesh=mesh,
        in_specs=(
            P(("groups", "users"), "seq", "heads"),
            P(("groups", "users"), "seq", "heads"),
            P(("groups", "users"), "seq", "heads"),
            P(("groups", "users")),
            P(("groups", "users"), None, "seq", None),
            P(("groups", "users"), None, "seq"),
            P("heads", None),
        ),
        out_specs=P(("groups", "users"), "seq", "heads"),
        check_vma=False,
    )
```

profile of v0, /device:TPU:0, one launch (start us, length us, event | category | flops | bytes accessed | tf_op | source)
XLA Modules:
  0.0 187.0 jit_solution(14279433392063117735)
XLA Ops:
  6.5 1.6 copy.99
  8.1 6.3 %copy.22 = bf16[4,2048,256]{1,2,0:T(8,128)(2,1)} copy(bf16[4,2048,256]{2,1,0:T(8,128)(2,1)} %param.14) | data formatting | bytes 8388608 | tf_op args[1]
  14.4 6.4 %copy.23 = bf16[4,2048,256]{1,2,0:T(8,128)(2,1)} copy(bf16[4,2048,256]{2,1,0:T(8,128)(2,1)} %param.15) | data formatting | bytes 8388608 | tf_op args[2]
  20.9 148.3 %while.130 = (s32[]{:T(128)}, bf16[4,64,256]{2,1,0:T(8,128)(2,1)}, f32[4,64,4]{1,2,0:T(4,128)S(1)}, f32[4,64,4]{1,2,0:T(4,128)S(1)}, f32[4,64,256]{1,2,0:T(8,128...) while((s32[]{:T(128)}, bf16[4,64,256]{2,1,0:T(8,128)(2,1)}, ...), condition=%wide.region_11.12_spmd, body=%wide.region_0.11_spmd.sunk | while | flops 278595616 | bytes 24837028 | solution.py:108
  20.9 3.1 %collective-permute-start = (bf16[4,64,256]{2,1,0:T(8,128)(2,1)}, bf16[4,64,256]{2,1,0:T(8,128)(2,1)S(1)}, u32[]{:S(2)}, u32[]{:S(2)}) collective-permute-start(bf16[4,64,256]{2,1,0:T(8,128)(2,1)} %get-tuple-element.1129), channel_id=1, source_target_pairs={{0,4},{4,8},{8,12},{12,0},{1,5},{5,9},{9,13},{13,1},{2,6},{6,10},{... | collective-permute-start | bytes 393224 | tf_op jit(solution)/shard_map/while/body/eval_jaxpr/ppermute | solution.py:13
  24.2 27.0 %while.132 = (s32[]{:T(128)}, f32[4,64,4]{1,2,0:T(4,128)S(1)}, f32[4,64,4]{1,2,0:T(4,128)S(1)}, f32[4,64,256]{1,2,0:T(8,128)S(1)}, s32[4,64,8]{1,2,0:T(8,128)S(1...) while((s32[]{:T(128)}, f32[4,64,4]{1,2,0:T(4,128)S(1)}, ...), condition=%wide.region_5.5_spmd, body=%wide.region_1.4_spmd.sunk | while | flops 139095040 | bytes 9696157 | solution.py:78
  26.8 1.8 fusion.76
  28.6 1.8 fusion.78
  33.5 1.8 fusion.76
  35.3 1.8 fusion.78
  40.2 1.8 fusion.76
  42.1 1.8 fusion.78
  47.0 1.8 fusion.76
  48.8 1.8 fusion.78
  51.3 1.6 collective-permute-start.6
  54.6 24.2 %while.131 = (s32[]{:T(128)}, f32[4,64,4]{1,2,0:T(4,128)S(1)}, f32[4,64,4]{1,2,0:T(4,128)S(1)}, f32[4,64,256]{1,2,0:T(8,128)S(1)}, s32[4,64,8]{1,2,0:T(8,128)S(1...) while((s32[]{:T(128)}, f32[4,64,4]{1,2,0:T(4,128)S(1)}, ...), condition=%wide.region_10.10_spmd, body=%wide.region_6.9_spmd.sunk | while | flops 139095040 | bytes 9696157 | solution.py:78
  56.5 1.8 fusion.69
  58.4 1.8 fusion.71
  62.6 1.8 fusion.69
  64.4 1.8 fusion.71
  68.6 1.8 fusion.69
  70.5 1.8 fusion.71
  74.7 1.8 fusion.69
  76.5 1.8 fusion.71
  79.0 1.8 collective-permute-start.7
  84.0 12.8 %collective-permute-done.4 = f32[4,64,4]{1,2,0:T(4,128)S(1)} collective-permute-done((f32[4,64,4]{1,2,0:T(4,128)S(1)}, f32[4,64,4]{1,2,0:T(4,128)S(1)}, u32[]{:S(2)}, u32[]{:S(2)}) %collective-permute-start.4) | collective-permute-done | bytes 4128 | tf_op jit(solution)/shard_map/while/body/eval_jaxpr/ppermute | solution.py:13
  97.1 27.0 %while.132 = (s32[]{:T(128)}, f32[4,64,4]{1,2,0:T(4,128)S(1)}, f32[4,64,4]{1,2,0:T(4,128)S(1)}, f32[4,64,256]{1,2,0:T(8,128)S(1)}, s32[4,64,8]{1,2,0:T(8,128)S(1...) while((s32[]{:T(128)}, f32[4,64,4]{1,2,0:T(4,128)S(1)}, ...), condition=%wide.region_5.5_spmd, body=%wide.region_1.4_spmd.sunk | while | flops 139095040 | bytes 9696157 | solution.py:78
  99.6 1.8 fusion.76
  101.5 1.8 fusion.78
  106.4 1.8 fusion.76
  108.2 1.8 fusion.78
  113.1 1.8 fusion.76
  114.9 1.8 fusion.78
  119.8 1.8 fusion.76
  121.7 1.8 fusion.78
  126.9 2.1 %collective-permute-start.3 = (f32[4,64,4]{1,2,0:T(4,128)S(1)}, f32[4,64,4]{1,2,0:T(4,128)S(1)}, u32[]{:S(2)}, u32[]{:S(2)}) collective-permute-start(f32[4,64,4]{1,2,0:T(4,128)S(1)} %bitcast.193), channel_id=1, source_target_pairs={{0,4},{4,8},{8,12},{12,0},{1,5},{5,9},{9,13},{13,1},{2,6},{6,10},{... | collective-permute-start | bytes 12296 | tf_op jit(solution)/shard_map/while/body/eval_jaxpr/ppermute | solution.py:13
  129.2 24.2 %while.131 = (s32[]{:T(128)}, f32[4,64,4]{1,2,0:T(4,128)S(1)}, f32[4,64,4]{1,2,0:T(4,128)S(1)}, f32[4,64,256]{1,2,0:T(8,128)S(1)}, s32[4,64,8]{1,2,0:T(8,128)S(1...) while((s32[]{:T(128)}, f32[4,64,4]{1,2,0:T(4,128)S(1)}, ...), condition=%wide.region_10.10_spmd, body=%wide.region_6.9_spmd.sunk | while | flops 139095040 | bytes 9696157 | solution.py:78
  131.1 1.8 fusion.69
  132.9 1.8 fusion.71
  137.1 1.8 fusion.69
  138.9 1.8 fusion.71
  143.2 1.8 fusion.69
  145.0 1.8 fusion.71
  149.2 1.8 fusion.69
  151.0 1.8 fusion.71
  156.3 2.2 %collective-permute-start.5 = (f32[4,64,4]{1,2,0:T(4,128)S(1)}, f32[4,64,4]{1,2,0:T(4,128)S(1)}, u32[]{:S(2)}, u32[]{:S(2)}) collective-permute-start(f32[4,64,4]{1,2,0:T(4,128)S(1)} %bitcast.197), channel_id=1, source_target_pairs={{0,4},{4,8},{8,12},{12,0},{1,5},{5,9},{9,13},{13,1},{2,6},{6,10},{... | collective-permute-start | bytes 12296 | tf_op jit(solution)/shard_map/while/body/eval_jaxpr/ppermute | solution.py:13
  158.5 10.7 %collective-permute-done.4 = f32[4,64,4]{1,2,0:T(4,128)S(1)} collective-permute-done((f32[4,64,4]{1,2,0:T(4,128)S(1)}, f32[4,64,4]{1,2,0:T(4,128)S(1)}, u32[]{:S(2)}, u32[]{:S(2)}) %collective-permute-start.4) | collective-permute-done | bytes 4128 | tf_op jit(solution)/shard_map/while/body/eval_jaxpr/ppermute | solution.py:13
  170.3 9.9 %reduce-scatter.2.cloned.1.call-done = bf16[4,64,256]{2,1,0:T(8,128)(2,1)} async-done(((bf16[4,64,512]{2,1,0:T(8,128)(2,1)}), bf16[4,64,256]{2,1,0:T(8,128)(2,1)}) %reduce-scatter.2.cloned.1.call-update) | async-done | bytes 131088 | tf_op jit(solution)/shard_map/reduce_scatter | solution.py:111
  (289 shorter events, 55.7 us)
Async XLA Ops:
  6.5 162.8 %copy-start = (bf16[256,512]{1,0:T(8,128)(2,1)S(1)}, bf16[256,512]{1,0:T(8,128)(2,1)}, u32[]{:S(2)}) copy-start(bf16[256,512]{1,0:T(8,128)(2,1)} %param.19) | copy-start | bytes 786436
  6.5 173.6 %reduce-scatter.2.cloned.1.call-start = ((), (), s32[]{:S(2)}) async-start(), calls=%async_computation.1 | async-start | bytes 393216 | tf_op jit(solution)/shard_map/reduce_scatter | solution.py:111
  14.4 6.4 %copy-start.2 = (s32[4,256,1]{1,2,0:T(1,128)S(1)}, s32[4,256,1]{1,2,0:T(1,128)}, u32[]{:S(2)}) copy-start(s32[4,256,1]{1,2,0:T(1,128)} %param.18) | copy-start | bytes 12292
  14.4 6.5 %copy-start.1 = (s32[4,256,1,8]{1,3,2,0:T(8,128)S(1)}, s32[4,256,1,8]{1,3,2,0:T(8,128)}, u32[]{:S(2)}) copy-start(s32[4,256,1,8]{1,3,2,0:T(8,128)} %param.17) | copy-start | bytes 98308
  14.4 6.5 %copy-start.3 = (s32[4]{0:T(128)S(1)}, s32[4]{0:T(128)}, u32[]{:S(2)}) copy-start(s32[4]{0:T(128)} %param.16) | copy-start | bytes 52
  20.9 33.6 %collective-permute-start = (bf16[4,64,256]{2,1,0:T(8,128)(2,1)}, bf16[4,64,256]{2,1,0:T(8,128)(2,1)S(1)}, u32[]{:S(2)}, u32[]{:S(2)}) collective-permute-start(bf16[4,64,256]{2,1,0:T(8,128)(2,1)} %get-tuple-element.1129), channel_id=1, source_target_pairs={{0,4},{4,8},{8,12},{12,0},{1,5},{5,9},{9,13},{13,1},{2,6},{6,10},{... | collective-permute-start | bytes 393224 | tf_op jit(solution)/shard_map/while/body/eval_jaxpr/ppermute | solution.py:13
  51.3 27.6 %collective-permute-start.6 = (f32[4,64,256]{1,2,0:T(8,128)S(1)}, f32[4,64,256]{1,2,0:T(8,128)S(1)}, u32[]{:S(2)}, u32[]{:S(2)}) collective-permute-start(f32[4,64,256]{1,2,0:T(8,128)S(1)} %fusion.63), channel_id=1, source_target_pairs={{0,4},{4,8},{8,12},{12,0},{1,5},{5,9},{9,13},{13,1},{2,6},{6,10},{... | collective-permute-start | bytes 786440 | tf_op jit(solution)/shard_map/while/body/eval_jaxpr/ppermute | solution.py:13
  52.9 25.9 %collective-permute-start.2 = (f32[4,64,4]{1,2,0:T(4,128)S(1)}, f32[4,64,4]{1,2,0:T(4,128)S(1)}, u32[]{:S(2)}, u32[]{:S(2)}) collective-permute-start(f32[4,64,4]{1,2,0:T(4,128)S(1)} %bitcast.194), channel_id=1, source_target_pairs={{0,4},{4,8},{8,12},{12,0},{1,5},{5,9},{9,13},{13,1},{2,6},{6,10},{... | collective-permute-start | bytes 12296 | tf_op jit(solution)/shard_map/while/body/eval_jaxpr/ppermute | solution.py:13
  54.5 24.3 %collective-permute-start.3 = (f32[4,64,4]{1,2,0:T(4,128)S(1)}, f32[4,64,4]{1,2,0:T(4,128)S(1)}, u32[]{:S(2)}, u32[]{:S(2)}) collective-permute-start(f32[4,64,4]{1,2,0:T(4,128)S(1)} %bitcast.193), channel_id=1, source_target_pairs={{0,4},{4,8},{8,12},{12,0},{1,5},{5,9},{9,13},{13,1},{2,6},{6,10},{... | collective-permute-start | bytes 12296 | tf_op jit(solution)/shard_map/while/body/eval_jaxpr/ppermute | solution.py:13
  79.0 17.8 %collective-permute-start.7 = (f32[4,64,256]{1,2,0:T(8,128)S(1)}, f32[4,64,256]{1,2,0:T(8,128)S(1)}, u32[]{:S(2)}, u32[]{:S(2)}) collective-permute-start(f32[4,64,256]{1,2,0:T(8,128)S(1)} %fusion.64), channel_id=1, source_target_pairs={{0,4},{4,8},{8,12},{12,0},{1,5},{5,9},{9,13},{13,1},{2,6},{6,10},{... | collective-permute-start | bytes 786440 | tf_op jit(solution)/shard_map/while/body/eval_jaxpr/ppermute | solution.py:13
  80.7 16.1 %collective-permute-start.1 = (bf16[4,64,256]{2,1,0:T(8,128)(2,1)S(1)}, bf16[4,64,256]{2,1,0:T(8,128)(2,1)}, u32[]{:S(2)}, u32[]{:S(2)}) collective-permute-start(bf16[4,64,256]{2,1,0:T(8,128)(2,1)S(1)} %get-tuple-element.1180), channel_id=1, source_target_pairs={{0,4},{4,8},{8,12},{12,0},{1,5},{5,9},{9,13},{13,1},{2,6},{6,10},{... | collective-permute-start | bytes 393224 | tf_op jit(solution)/shard_map/while/body/eval_jaxpr/ppermute | solution.py:13
  82.3 14.4 %collective-permute-start.4 = (f32[4,64,4]{1,2,0:T(4,128)S(1)}, f32[4,64,4]{1,2,0:T(4,128)S(1)}, u32[]{:S(2)}, u32[]{:S(2)}) collective-permute-start(f32[4,64,4]{1,2,0:T(4,128)S(1)} %bitcast.198), channel_id=1, source_target_pairs={{0,4},{4,8},{8,12},{12,0},{1,5},{5,9},{9,13},{13,1},{2,6},{6,10},{... | collective-permute-start | bytes 12296 | tf_op jit(solution)/shard_map/while/body/eval_jaxpr/ppermute | solution.py:13
  83.9 12.9 %collective-permute-start.5 = (f32[4,64,4]{1,2,0:T(4,128)S(1)}, f32[4,64,4]{1,2,0:T(4,128)S(1)}, u32[]{:S(2)}, u32[]{:S(2)}) collective-permute-start(f32[4,64,4]{1,2,0:T(4,128)S(1)} %bitcast.197), channel_id=1, source_target_pairs={{0,4},{4,8},{8,12},{12,0},{1,5},{5,9},{9,13},{13,1},{2,6},{6,10},{... | collective-permute-start | bytes 12296 | tf_op jit(solution)/shard_map/while/body/eval_jaxpr/ppermute | solution.py:13
  96.8 32.3 %collective-permute-start = (bf16[4,64,256]{2,1,0:T(8,128)(2,1)}, bf16[4,64,256]{2,1,0:T(8,128)(2,1)S(1)}, u32[]{:S(2)}, u32[]{:S(2)}) collective-permute-start(bf16[4,64,256]{2,1,0:T(8,128)(2,1)} %get-tuple-element.1129), channel_id=1, source_target_pairs={{0,4},{4,8},{8,12},{12,0},{1,5},{5,9},{9,13},{13,1},{2,6},{6,10},{... | collective-permute-start | bytes 393224 | tf_op jit(solution)/shard_map/while/body/eval_jaxpr/ppermute | solution.py:13
  124.2 29.2 %collective-permute-start.6 = (f32[4,64,256]{1,2,0:T(8,128)S(1)}, f32[4,64,256]{1,2,0:T(8,128)S(1)}, u32[]{:S(2)}, u32[]{:S(2)}) collective-permute-start(f32[4,64,256]{1,2,0:T(8,128)S(1)} %fusion.63), channel_id=1, source_target_pairs={{0,4},{4,8},{8,12},{12,0},{1,5},{5,9},{9,13},{13,1},{2,6},{6,10},{... | collective-permute-start | bytes 786440 | tf_op jit(solution)/shard_map/while/body/eval_jaxpr/ppermute | solution.py:13
  125.4 28.0 %collective-permute-start.2 = (f32[4,64,4]{1,2,0:T(4,128)S(1)}, f32[4,64,4]{1,2,0:T(4,128)S(1)}, u32[]{:S(2)}, u32[]{:S(2)}) collective-permute-start(f32[4,64,4]{1,2,0:T(4,128)S(1)} %bitcast.194), channel_id=1, source_target_pairs={{0,4},{4,8},{8,12},{12,0},{1,5},{5,9},{9,13},{13,1},{2,6},{6,10},{... | collective-permute-start | bytes 12296 | tf_op jit(solution)/shard_map/while/body/eval_jaxpr/ppermute | solution.py:13
  126.9 26.4 %collective-permute-start.3 = (f32[4,64,4]{1,2,0:T(4,128)S(1)}, f32[4,64,4]{1,2,0:T(4,128)S(1)}, u32[]{:S(2)}, u32[]{:S(2)}) collective-permute-start(f32[4,64,4]{1,2,0:T(4,128)S(1)} %bitcast.193), channel_id=1, source_target_pairs={{0,4},{4,8},{8,12},{12,0},{1,5},{5,9},{9,13},{13,1},{2,6},{6,10},{... | collective-permute-start | bytes 12296 | tf_op jit(solution)/shard_map/while/body/eval_jaxpr/ppermute | solution.py:13
  153.5 15.8 %collective-permute-start.7 = (f32[4,64,256]{1,2,0:T(8,128)S(1)}, f32[4,64,256]{1,2,0:T(8,128)S(1)}, u32[]{:S(2)}, u32[]{:S(2)}) collective-permute-start(f32[4,64,256]{1,2,0:T(8,128)S(1)} %fusion.64), channel_id=1, source_target_pairs={{0,4},{4,8},{8,12},{12,0},{1,5},{5,9},{9,13},{13,1},{2,6},{6,10},{... | collective-permute-start | bytes 786440 | tf_op jit(solution)/shard_map/while/body/eval_jaxpr/ppermute | solution.py:13
  153.6 15.6 %collective-permute-start.1 = (bf16[4,64,256]{2,1,0:T(8,128)(2,1)S(1)}, bf16[4,64,256]{2,1,0:T(8,128)(2,1)}, u32[]{:S(2)}, u32[]{:S(2)}) collective-permute-start(bf16[4,64,256]{2,1,0:T(8,128)(2,1)S(1)} %get-tuple-element.1180), channel_id=1, source_target_pairs={{0,4},{4,8},{8,12},{12,0},{1,5},{5,9},{9,13},{13,1},{2,6},{6,10},{... | collective-permute-start | bytes 393224 | tf_op jit(solution)/shard_map/while/body/eval_jaxpr/ppermute | solution.py:13
  154.8 14.4 %collective-permute-start.4 = (f32[4,64,4]{1,2,0:T(4,128)S(1)}, f32[4,64,4]{1,2,0:T(4,128)S(1)}, u32[]{:S(2)}, u32[]{:S(2)}) collective-permute-start(f32[4,64,4]{1,2,0:T(4,128)S(1)} %bitcast.198), channel_id=1, source_target_pairs={{0,4},{4,8},{8,12},{12,0},{1,5},{5,9},{9,13},{13,1},{2,6},{6,10},{... | collective-permute-start | bytes 12296 | tf_op jit(solution)/shard_map/while/body/eval_jaxpr/ppermute | solution.py:13
  156.3 12.9 %collective-permute-start.5 = (f32[4,64,4]{1,2,0:T(4,128)S(1)}, f32[4,64,4]{1,2,0:T(4,128)S(1)}, u32[]{:S(2)}, u32[]{:S(2)}) collective-permute-start(f32[4,64,4]{1,2,0:T(4,128)S(1)} %bitcast.197), channel_id=1, source_target_pairs={{0,4},{4,8},{8,12},{12,0},{1,5},{5,9},{9,13},{13,1},{2,6},{6,10},{... | collective-permute-start | bytes 12296 | tf_op jit(solution)/shard_map/while/body/eval_jaxpr/ppermute | solution.py:13
Sparse Core Ops, SparseCore 0:
  170.4 9.7 reduce-scatter.1
where the time goes:
time: 189 us; the launch traced here: 187 us
  matrix products  59 us (31%)
  local copies, waits for them, and re-layouts  38 us (20%)
  waiting for transfers between devices  33.5 us (18%)
  starting transfers between devices  21.3 us (11%)
  other arithmetic  20.3 us (11%)
  between operations  13.4 us (7%)
    dot_general x16, matrix products, per_user(): jnp.einsum('rhd,ehd->rhe', query_split, key_user, preferred_element_type=...  29.3 us
    dot_general x16, matrix products, per_user(): jnp.einsum('rhe,ehd->rhd', weight.astype(jnp.bfloat16), value_user, prefe...  28.7 us
    ppermute x16, waiting for transfers between devices, passed_along(): return lax.ppermute(value, axis, pairs)  23.6 us
    ppermute x16, starting transfers between devices, passed_along(): return lax.ppermute(value, axis, pairs)  21.3 us
    dynamic_slice x32, local copies, waits for them, and re-layouts, local_part(): lax.map(per_user, (query_block, key_heads, value_heads, hist_len, id_bloc...  16 us
    unnamed x12, local copies, waits for them, and re-layouts  14.3 us
    reduce_scatter x1, waiting for transfers between devices, body(): lax.psum_scatter(projected.astype(jnp.bfloat16), 'heads', scatter_dimensi...  9.88 us
    lt x16, other arithmetic, shard_mask(): return event_chosen & (position < length)[None, :]  9.58 us
  transfers between devices with their start and end apart: 17, of which 5 were waited for; matrix products, arithmetic and copies ran while one was open for 54% of the time, Pallas kernels for 0%

commit v1 on v0

--- a/solution.py
+++ b/solution.py
@@ -1,6 +1,10 @@
+import functools
+
 import jax
 import jax.numpy as jnp
 from jax import lax
+from jax.experimental import pallas as pl
+from jax.experimental.pallas import tpu as pltpu
 from jax.sharding import PartitionSpec as P
 
 HD = 64
@@ -36,7 +40,7 @@
     return (peak_score, weight_sum, weighted)
 
 
-def body(queries, keys, values, hist_len, block_ids, block_count, out_weight):
+def ring_body(queries, keys, values, hist_len, block_ids, block_count, out_weight):
     user_count = queries.shape[0]
     visit_rows = queries.shape[1]
     feature_width = queries.shape[2]
@@ -114,6 +118,334 @@
     return joined
 
 
+LANES = 128
+CHUNK = 256
+FAR = -32768.0
+MESH = pl.DeviceIdType.MESH
+
+
+def kernel(
+    seq_size, head_size, q_ref, k_hbm, v_hbm, id_ref, count_ref, length_ref, w_ref, out_ref,
+    q_all, k_buf, v_buf, mask, place, scores, lse_send, lse_recv, lse_turn, o_send, o_recv,
+    p_own, p_send, p_recv,
+    kv_sem, q_send_sem, q_recv_sem, o_send_sem, o_recv_sem, l_send_sem, l_recv_sem,
+    p_send_sem, p_recv_sem,
+):
+    users, rows, width = q_ref.shape
+    cands = q_all.shape[1]
+    events = k_buf.shape[1]
+    heads = width // HD
+    blocks = events // BLOCK
+    me = lax.axis_index("seq")
+    hx = lax.axis_index("heads")
+
+    def kv_copy(u, which):
+        src, dst = ((k_hbm, k_buf), (v_hbm, v_buf))[which]
+        return pltpu.make_async_copy(src.at[u], dst.at[u], kv_sem.at[u, which])
+
+    def row_range(s):
+        return pl.ds(pl.multiple_of(s * rows, rows), rows)
+
+    def q_copy(u, block, way, own=False):
+        target = me + 1 if way == 0 else me - 1
+        return pltpu.make_async_remote_copy(
+            src_ref=q_ref.at[u] if own else q_all.at[u, row_range(block)],
+            dst_ref=q_all.at[u, row_range(block)],
+            send_sem=q_send_sem.at[u, way, block],
+            recv_sem=q_recv_sem.at[u, block],
+            device_id={"seq": target},
+            device_id_type=MESH,
+        )
+
+    def o_copy(u, j):
+        to = lax.rem(me + j, seq_size)
+        return pltpu.make_async_remote_copy(
+            src_ref=o_send.at[u, row_range(to)],
+            dst_ref=o_recv.at[u, me],
+            send_sem=o_send_sem.at[u, j],
+            recv_sem=o_recv_sem.at[u, j],
+            device_id={"seq": to},
+            device_id_type=MESH,
+        )
+
+    def l_copy(u, j):
+        to = lax.rem(me + j, seq_size)
+        return pltpu.make_async_remote_copy(
+            src_ref=lse_send.at[u],
+            dst_ref=lse_recv.at[u, me],
+            send_sem=l_send_sem.at[u, j],
+            recv_sem=l_recv_sem.at[u, j],
+            device_id={"seq": to},
+            device_id_type=MESH,
+        )
+
+    def p_copy(u, j):
+        return pltpu.make_async_remote_copy(
+            src_ref=p_send.at[u, j],
+            dst_ref=p_recv.at[u, j],
+            send_sem=p_send_sem.at[u, j],
+            recv_sem=p_recv_sem.at[u, j],
+            device_id={"heads": lax.rem(hx + j, head_size)},
+            device_id_type=MESH,
+        )
+
+    def each_user(step):
+        def run(u, carry):
+            step(u)
+            return carry
+
+        lax.fori_loop(0, users, run, 0)
+
+    @each_user
+    def _(u):
+        kv_copy(u, 0).start()
+        kv_copy(u, 1).start()
+
+    barrier = pltpu.get_barrier_semaphore()
+    for j in range(1, seq_size):
+        pl.semaphore_signal(
+            barrier, inc=1, device_id={"seq": lax.rem(me + j, seq_size)}, device_id_type=MESH
+        )
+    for j in range(1, head_size):
+        pl.semaphore_signal(
+            barrier, inc=1, device_id={"heads": lax.rem(hx + j, head_size)}, device_id_type=MESH
+        )
+    pl.semaphore_wait(barrier, seq_size + head_size - 2)
+
+    @each_user
+    def _(u):
+        @pl.when(me < seq_size - 1)
+        def _():
+            q_copy(u, me, 0, own=True).start()
+
+        @pl.when(me > 0)
+        def _():
+            q_copy(u, me, 1, own=True).start()
+
+    def q_round(u, r):
+        @pl.when(me - r >= 0)
+        def _():
+            q_copy(u, me - r, 0).wait_recv()
+
+            @pl.when(me < seq_size - 1)
+            def _():
+                q_copy(u, me - r, 0).start()
+
+        @pl.when(me + r < seq_size)
+        def _():
+            q_copy(u, me + r, 1).wait_recv()
+
+            @pl.when(me > 0)
+            def _():
+                q_copy(u, me + r, 1).start()
+
+    lane = lax.broadcasted_iota(jnp.int32, (cands, LANES), 1)
+
+    @each_user
+    def _(u):
+        q_all[u, row_range(me), :] = q_ref[u]
+        chosen = jnp.zeros((cands, LANES), jnp.bool_)
+        ids = id_ref[u]
+        count = count_ref[u]
+        for i in range(ids.shape[1]):
+            chosen = chosen | ((ids[:, i : i + 1] == lane) & (count > i))
+        mask[u] = jnp.where(chosen | (lane > blocks), 0.0, FAR).astype(jnp.bfloat16)
+
+    def placed(u):
+        event = lax.broadcasted_iota(jnp.int32, (events, LANES), 0)
+        column = lax.broadcasted_iota(jnp.int32, (events, LANES), 1)
+        past = me * events + event >= length_ref[u]
+        here = (event // BLOCK == column) | ((column == blocks) & past)
+        place[...] = jnp.where(here, 1.0, 0.0).astype(jnp.bfloat16)
+
+    for r in range(1, seq_size):
+        q_round(0, r)
+
+    def attend(u):
+        placed(u)
+        kv_copy(u, 0).wait()
+        kv_copy(u, 1).wait()
+        q_user = q_all[u]
+        peak_all = jnp.zeros((cands, LANES), jnp.float32)
+        sum_all = jnp.ones((cands, LANES), jnp.float32)
+        per_head = -(-(seq_size - 1) // heads)
+        outs = []
+        for h in range(heads):
+            for r in range(1 + h * per_head, min(seq_size, 1 + (h + 1) * per_head)):
+
+                @pl.when(u + 1 < users)
+                def _(r=r):
+                    q_round(u + 1, r)
+
+            pair = slice(h // 2 * LANES, h // 2 * LANES + LANES)
+            half = (lane // HD) == (h % 2)
+            q_head = jnp.where(half, q_user[:, pair] * (HD ** -0.5), 0.0).astype(jnp.bfloat16)
+            q_wide = jnp.concatenate([q_head, mask[u]], axis=1)
+            best = jnp.full((cands, LANES), 2 * FAR, jnp.float32)
+            for e in range(0, events, CHUNK):
+                k_wide = jnp.concatenate(
+                    [k_buf[u, e : e + CHUNK, pair], place[e : e + CHUNK]], axis=1
+                )
+                part = lax.dot_general(
+                    q_wide, k_wide, (((1,), (1,)), ((), ())), preferred_element_type=jnp.float32
+                )
+                scores[h % 2, :, e : e + CHUNK] = part
+                for c in range(0, CHUNK, LANES):
+                    best = jnp.maximum(best, part[:, c : c + LANES])
+            peak = jnp.max(best, axis=1, keepdims=True)
+            total = jnp.zeros((cands, 2 * LANES), jnp.float32)
+            for e in range(0, events, CHUNK):
+                weight = jnp.exp(scores[h % 2, :, e : e + CHUNK] - peak).astype(jnp.bfloat16)
+                v_wide = jnp.concatenate(
+                    [v_buf[u, e : e + CHUNK, pair], jnp.ones((CHUNK, LANES), jnp.bfloat16)], axis=1
+                )
+                total = total + jnp.dot(weight, v_wide, preferred_element_type=jnp.float32)
+            weight_sum = total[:, LANES:]
+            normal = total[:, :LANES] / weight_sum
+            outs.append(normal)
+            peak_all = jnp.where(lane == h, peak, peak_all)
+            sum_all = jnp.where(lane == h, weight_sum, sum_all)
+            if h % 2 == 1:
+                joined_pair = jnp.where(lane < HD, outs[h - 1], outs[h]).astype(jnp.bfloat16)
+                o_send[u, :, pair] = joined_pair
+        lse = peak_all + jnp.log(sum_all)
+        lse_send[u] = lse.T[:8]
+        lse_recv[u, me] = lse_send[u]
+        o_recv[u, me] = o_send[u, row_range(me), :]
+        for j in range(1, seq_size):
+            o_copy(u, j).start()
+            l_copy(u, j).start()
+
+    def combine(u):
+        for j in range(1, seq_size):
+            o_copy(u, j).wait_recv()
+            l_copy(u, j).wait_recv()
+        flat = jnp.concatenate([lse_recv[u, s] for s in range(seq_size)], axis=0)
+        flat = jnp.pad(flat, ((0, -flat.shape[0] % LANES), (0, 0)))
+        lse_turn[...] = flat.T
+        mine = lse_turn[row_range(me), :]
+        first = lax.broadcasted_iota(jnp.int32, (rows, LANES), 1) < HD
+        attended = []
+        for h in range(0, heads, 2):
+            pair = slice(h // 2 * LANES, h // 2 * LANES + LANES)
+            lses = [
+                jnp.where(first, mine[:, 8 * s + h : 8 * s + h + 1], mine[:, 8 * s + h + 1 : 8 * s + h + 2])
+                for s in range(seq_size)
+            ]
+            top = functools.reduce(jnp.maximum, lses)
+            numer = jnp.zeros((rows, LANES), jnp.float32)
+            denom = jnp.zeros((rows, LANES), jnp.float32)
+            for s in range(seq_size):
+                share = jnp.exp(lses[s] - top)
+                numer = numer + share * o_recv[u, s, :, pair].astype(jnp.float32)
+                denom = denom + share
+            attended.append((numer / denom).astype(jnp.bfloat16))
+        attended = jnp.concatenate(attended, axis=1)
+        for j in list(range(1, head_size)) + [0]:
+            first_column = pl.multiple_of(lax.rem(hx + j, head_size) * width, width)
+            part = jnp.dot(
+                attended, w_ref[:, pl.ds(first_column, width)], preferred_element_type=jnp.float32
+            )
+            if j:
+                p_send[u, j] = part.astype(jnp.bfloat16)
+                p_copy(u, j).start()
+            else:
+                p_own[u] = part
+
+    def finish(u):
+        total = p_own[u]
+        for j in range(1, head_size):
+            p_copy(u, j).wait_recv()
+            total = total + p_recv[u, j].astype(jnp.float32)
+        out_ref[u] = total.astype(jnp.bfloat16)
+
+    def stage(t, carry):
+        @pl.when(t < users)
+        def _():
+            attend(t)
+
+        @pl.when((t >= 1) & (t <= users))
+        def _():
+            combine(t - 1)
+
+        @pl.when(t >= 2)
+        def _():
+            finish(t - 2)
+
+        return carry
+
+    lax.fori_loop(0, users + 2, stage, 0)
+
+    @each_user
+    def _(u):
+        for j in range(1, seq_size):
+            o_copy(u, j).wait_send()
+            l_copy(u, j).wait_send()
+        for j in range(1, head_size):
+            p_copy(u, j).wait_send()
+        for s in range(seq_size):
+
+            @pl.when((me < seq_size - 1) & (s <= me))
+            def _(s=s):
+                q_copy(u, s, 0).wait_send()
+
+            @pl.when((me > 0) & (s >= me))
+            def _(s=s):
+                q_copy(u, s, 1).wait_send()
+
+
+def body(queries, keys, values, hist_len, block_ids, block_count, out_weight):
+    users, rows, width = queries.shape
+    events = keys.shape[1]
+    slots = block_ids.shape[3]
+    seq_size = lax.axis_size("seq")
+    head_size = lax.axis_size("heads")
+    cands = block_ids.shape[1]
+    if rows % 16 or width % LANES or events % CHUNK or 8 * seq_size > LANES:
+        return ring_body(queries, keys, values, hist_len, block_ids, block_count, out_weight)
+    vmem = pl.BlockSpec(memory_space=pltpu.VMEM)
+    hbm = pl.BlockSpec(memory_space=pl.ANY)
+    bf16, f32 = jnp.bfloat16, jnp.float32
+    dma = pltpu.SemaphoreType.DMA
+    return pl.pallas_call(
+        functools.partial(kernel, seq_size, head_size),
+        out_shape=jax.ShapeDtypeStruct(queries.shape, bf16),
+        in_specs=[vmem, hbm, hbm, vmem, vmem, pl.BlockSpec(memory_space=pltpu.SMEM), vmem],
+        out_specs=vmem,
+        scratch_shapes=[
+            pltpu.VMEM((users, cands, width), bf16),
+            pltpu.VMEM((users, events, width), bf16),
+            pltpu.VMEM((users, events, width), bf16),
+            pltpu.VMEM((users, cands, LANES), bf16),
+            pltpu.VMEM((events, LANES), bf16),
+            pltpu.VMEM((2, cands, events), f32),
+            pltpu.VMEM((users, 8, cands), f32),
+            pltpu.VMEM((users, seq_size, 8, cands), f32),
+            pltpu.VMEM((cands, LANES), f32),
+            pltpu.VMEM((users, cands, width), bf16),
+            pltpu.VMEM((users, seq_size, rows, width), bf16),
+            pltpu.VMEM((users, rows, width), f32),
+            pltpu.VMEM((users, head_size, rows, width), bf16),
+            pltpu.VMEM((users, head_size, rows, width), bf16),
+            dma((users, 2)),
+            dma((users, 2, seq_size)),
+            dma((users, seq_size)),
+            dma((users, seq_size)),
+            dma((users, seq_size)),
+            dma((users, seq_size)),
+            dma((users, seq_size)),
+            dma((users, head_size)),
+            dma((users, head_size)),
+        ],
+        compiler_params=pltpu.CompilerParams(
+            collective_id=0, has_side_effects=True, vmem_limit_bytes=48 * 1024 * 1024
+        ),
+    )(
+        queries, keys, values, block_ids.reshape(users, cands, slots),
+        block_count.reshape(users, cands, 1), hist_len, out_weight,
+    )
+
+
 def solution(mesh):
     return jax.shard_map(
         body,

time: 189 us -> 58.4 us (0.31)
  matrix products: 59 us -> 0 us
  Pallas kernels: 0 us -> 50.9 us
  waiting for transfers between devices: 33.5 us -> 0 us
  local copies, waits for them, and re-layouts: 38 us -> 7.21 us
  starting transfers between devices: 21.3 us -> 0 us
  other arithmetic: 20.3 us -> 0 us
  between operations: 13.4 us -> 0.04 us
    dot_general x33 -> x0, matrix products: 59 us -> none  [the longest x16 29.3 us: per_user(): jnp.einsum('rhd,ehd->rhe', query_split, key_user, preferred_element_type=...]
    pallas_call x0 -> x1, Pallas kernels: none -> 50.9 us  [body(): pl.pallas_call(functools.partial(kernel, seq_size, head_size), out_shape=...]
    ppermute x16 -> x0, waiting for transfers between devices: 23.6 us -> none  [passed_along(): return lax.ppermute(value, axis, pairs)]
    ppermute x16 -> x0, starting transfers between devices: 21.3 us -> none  [passed_along(): return lax.ppermute(value, axis, pairs)]
    dynamic_slice x36 -> x0, local copies, waits for them, and re-layouts: 16.3 us -> none  [the longest x32 16 us: local_part(): lax.map(per_user, (query_block, key_heads, value_heads, hist_len, id_bloc...]
    reduce_scatter x1 -> x0, waiting for transfers between devices: 9.88 us -> none  [body(): lax.psum_scatter(projected.astype(jnp.bfloat16), 'heads', scatter_dimensi...]
    lt x32 -> x0, other arithmetic: 9.69 us -> none  [the longest x16 9.58 us: shard_mask(): return event_chosen & (position < length)[None, :]]
    reduce_sum x16 -> x0, other arithmetic: 8.47 us -> none  [per_user(): weight_sum = jnp.sum(weight, axis=2)]
  transfers between devices with their start and end apart: 17 -> 0, of which waited for: 5 -> 0; matrix products, arithmetic and copies ran while one was open for 54% -> 0% of each run, Pallas kernels for 0% -> 0%
where the time goes in v1:
time: 58.4 us; the launch traced here: 58.1 us
  Pallas kernels  50.9 us (87%)
  local copies, waits for them, and re-layouts  7.21 us (12%)
    pallas_call x1, Pallas kernels, body(): pl.pallas_call(functools.partial(kernel, seq_size, head_size), out_shape=...  50.9 us
    unnamed x11, local copies, waits for them, and re-layouts  7.21 us

profile of v1, /device:TPU:0, one launch (start us, length us, event | category | flops | bytes accessed | tf_op | source)
XLA Modules:
  0.0 58.1 jit_solution(10029296303955649688)
XLA Ops:
  0.0 0.9 %copy.8 = s32[4,256,1,8]{3,1,0,2:T(8,128)S(1)} copy(s32[4,256,1,8]{1,3,2,0:T(8,128)} %param.11) | data formatting | bytes 65536 | tf_op args[4]
  1.0 0.9 %copy.9.count_ref = s32[4,256,1]{2,1,0:T(8,128)S(1)} copy(s32[4,256,1]{1,2,0:T(1,128)} %param.12) | data formatting | bytes 8192 | tf_op args[5]
  1.9 0.0 copy-start
  1.9 2.2 %copy-done = bf16[4,2048,256]{2,1,0:T(8,128)(2,1)S(1)} copy-done((bf16[4,2048,256]{2,1,0:T(8,128)(2,1)S(1)}, bf16[4,2048,256]{2,1,0:T(8,128)(2,1)}, u32[]{:S(2)}) %copy-start) | copy-done | bytes 4194328
  4.1 0.0 copy-start.1
  4.1 0.9 %copy-done.1 = bf16[256,512]{1,0:T(8,128)(2,1)S(1)} copy-done((bf16[256,512]{1,0:T(8,128)(2,1)S(1)}, bf16[256,512]{1,0:T(8,128)(2,1)}, u32[]{:S(2)}) %copy-start.1) | copy-done | bytes 262168
  5.0 0.0 copy-start.2
  5.0 0.9 %copy-done.2 = bf16[4,64,256]{2,1,0:T(8,128)(2,1)S(1)} copy-done((bf16[4,64,256]{2,1,0:T(8,128)(2,1)S(1)}, bf16[4,64,256]{2,1,0:T(8,128)(2,1)}, u32[]{:S(2)}) %copy-start.2) | copy-done | bytes 131096
  5.9 0.0 copy-start.3
  5.9 0.7 %copy-done.3 = s32[4]{0:T(128)S(1)} copy-done((s32[4]{0:T(128)S(1)}, s32[4]{0:T(128)}, u32[]{:S(2)}) %copy-start.3) | copy-done | bytes 40
  6.6 50.9 %shard_map.73 = bf16[4,64,256]{2,1,0:T(8,128)(2,1)S(1)} custom-call(bf16[4,64,256]{2,1,0:T(8,128)(2,1)S(1)} %copy-done.2, bf16[4,2048,256]{2,1,0:T(8,128)(2,1)S(1)} %copy-done, bf16[4,2048,256]{2,1,0:T(8,128)(2,1)} %v_hbm.1, s32[4,256,8]{2,1,0:T(8,128)S(1)} %bitcast.1, s32[4,256,1]{2,1,0:T(8,128)S(1)} %copy.9.count_ref, s32[4]{0:T(128)S(1)} %copy-done.3, ...), custom_call_target="tpu_custom_call" | custom-call | tf_op jit(solution)/shard_map/pallas_call | solution.py:410
  57.4 0.7 %copy.11 = bf16[4,64,256]{2,1,0:T(8,128)(2,1)} copy(bf16[4,64,256]{2,1,0:T(8,128)(2,1)S(1)} %shard_map.73) | data formatting | bytes 262144
Async XLA Ops:
  1.9 2.2 %copy-start = (bf16[4,2048,256]{2,1,0:T(8,128)(2,1)S(1)}, bf16[4,2048,256]{2,1,0:T(8,128)(2,1)}, u32[]{:S(2)}) copy-start(bf16[4,2048,256]{2,1,0:T(8,128)(2,1)} %k_hbm.1) | copy-start | bytes 12582916
  4.1 0.9 %copy-start.1 = (bf16[256,512]{1,0:T(8,128)(2,1)S(1)}, bf16[256,512]{1,0:T(8,128)(2,1)}, u32[]{:S(2)}) copy-start(bf16[256,512]{1,0:T(8,128)(2,1)} %w_ref.1) | copy-start | bytes 786436
  5.0 0.9 %copy-start.2 = (bf16[4,64,256]{2,1,0:T(8,128)(2,1)S(1)}, bf16[4,64,256]{2,1,0:T(8,128)(2,1)}, u32[]{:S(2)}) copy-start(bf16[4,64,256]{2,1,0:T(8,128)(2,1)} %q_ref.1) | copy-start | bytes 393220
  5.9 0.7 %copy-start.3 = (s32[4]{0:T(128)S(1)}, s32[4]{0:T(128)}, u32[]{:S(2)}) copy-start(s32[4]{0:T(128)} %length_ref.1) | copy-start | bytes 52

commit v2 on v1

--- a/solution.py
+++ b/solution.py
@@ -125,13 +125,13 @@
 
 
 def kernel(
-    seq_size, head_size, q_ref, k_hbm, v_hbm, id_ref, count_ref, length_ref, w_ref, out_ref,
-    q_all, k_buf, v_buf, mask, place, scores, lse_send, lse_recv, lse_turn, o_send, o_recv,
+    seq_size, head_size, q_hbm, k_hbm, v_hbm, id_ref, count_ref, length_ref, w_hbm, out_ref,
+    q_all, w_ref, k_buf, v_buf, mask, place, scores, lse_send, lse_recv, lse_turn, o_send, o_recv,
     p_own, p_send, p_recv,
-    kv_sem, q_send_sem, q_recv_sem, o_send_sem, o_recv_sem, l_send_sem, l_recv_sem,
+    kv_sem, q_own_sem, w_sem, q_send_sem, q_recv_sem, o_send_sem, o_recv_sem, l_send_sem, l_recv_sem,
     p_send_sem, p_recv_sem,
 ):
-    users, rows, width = q_ref.shape
+    users, rows, width = q_hbm.shape
     cands = q_all.shape[1]
     events = k_buf.shape[1]
     heads = width // HD
@@ -146,14 +146,13 @@
     def row_range(s):
         return pl.ds(pl.multiple_of(s * rows, rows), rows)
 
-    def q_copy(u, block, way, own=False):
-        target = me + 1 if way == 0 else me - 1
+    def q_copy(u, j):
         return pltpu.make_async_remote_copy(
-            src_ref=q_ref.at[u] if own else q_all.at[u, row_range(block)],
-            dst_ref=q_all.at[u, row_range(block)],
-            send_sem=q_send_sem.at[u, way, block],
-            recv_sem=q_recv_sem.at[u, block],
-            device_id={"seq": target},
+            src_ref=q_hbm.at[u],
+            dst_ref=q_all.at[u, row_range(me)],
+            send_sem=q_send_sem.at[u, j],
+            recv_sem=q_recv_sem.at[u, j],
+            device_id={"seq": lax.rem(me + j, seq_size)},
             device_id_type=MESH,
         )
 
@@ -171,13 +170,16 @@
     def l_copy(u, j):
         to = lax.rem(me + j, seq_size)
         return pltpu.make_async_remote_copy(
-            src_ref=lse_send.at[u],
+            src_ref=lse_send.at[u, to * rows // LANES],
             dst_ref=lse_recv.at[u, me],
             send_sem=l_send_sem.at[u, j],
             recv_sem=l_recv_sem.at[u, j],
             device_id={"seq": to},
             device_id_type=MESH,
         )
+
+    def q_own(u):
+        return pltpu.make_async_copy(q_hbm.at[u], q_all.at[u, row_range(me)], q_own_sem.at[u])
 
     def p_copy(u, j):
         return pltpu.make_async_remote_copy(
@@ -198,8 +200,12 @@
 
     @each_user
     def _(u):
+        q_own(u).start()
         kv_copy(u, 0).start()
         kv_copy(u, 1).start()
+
+    w_copy = pltpu.make_async_copy(w_hbm, w_ref, w_sem)
+    w_copy.start()
 
     barrier = pltpu.get_barrier_semaphore()
     for j in range(1, seq_size):
@@ -214,73 +220,39 @@
 
     @each_user
     def _(u):
-        @pl.when(me < seq_size - 1)
-        def _():
-            q_copy(u, me, 0, own=True).start()
-
-        @pl.when(me > 0)
-        def _():
-            q_copy(u, me, 1, own=True).start()
-
-    def q_round(u, r):
-        @pl.when(me - r >= 0)
-        def _():
-            q_copy(u, me - r, 0).wait_recv()
-
-            @pl.when(me < seq_size - 1)
-            def _():
-                q_copy(u, me - r, 0).start()
-
-        @pl.when(me + r < seq_size)
-        def _():
-            q_copy(u, me + r, 1).wait_recv()
-
-            @pl.when(me > 0)
-            def _():
-                q_copy(u, me + r, 1).start()
+        for j in range(1, seq_size):
+            q_copy(u, j).start()
 
     lane = lax.broadcasted_iota(jnp.int32, (cands, LANES), 1)
 
-    @each_user
-    def _(u):
-        q_all[u, row_range(me), :] = q_ref[u]
-        chosen = jnp.zeros((cands, LANES), jnp.bool_)
-        ids = id_ref[u]
-        count = count_ref[u]
-        for i in range(ids.shape[1]):
-            chosen = chosen | ((ids[:, i : i + 1] == lane) & (count > i))
-        mask[u] = jnp.where(chosen | (lane > blocks), 0.0, FAR).astype(jnp.bfloat16)
-
-    def placed(u):
+    def prepare(u):
+        block = lax.broadcasted_iota(jnp.int32, (LANES, cands), 0)
+        chosen = block > blocks
+        for i in range(id_ref.shape[1]):
+            chosen = chosen | ((id_ref[u, i : i + 1] == block) & (count_ref[u] > i))
+        mask[...] = jnp.where(chosen, 0.0, FAR).T.astype(jnp.bfloat16)
         event = lax.broadcasted_iota(jnp.int32, (events, LANES), 0)
         column = lax.broadcasted_iota(jnp.int32, (events, LANES), 1)
         past = me * events + event >= length_ref[u]
         here = (event // BLOCK == column) | ((column == blocks) & past)
         place[...] = jnp.where(here, 1.0, 0.0).astype(jnp.bfloat16)
 
-    for r in range(1, seq_size):
-        q_round(0, r)
-
+    prepare(0)
     def attend(u):
-        placed(u)
+        q_own(u).wait()
+        for j in range(1, seq_size):
+            q_copy(u, j).wait_recv()
         kv_copy(u, 0).wait()
         kv_copy(u, 1).wait()
         q_user = q_all[u]
         peak_all = jnp.zeros((cands, LANES), jnp.float32)
         sum_all = jnp.ones((cands, LANES), jnp.float32)
-        per_head = -(-(seq_size - 1) // heads)
         outs = []
         for h in range(heads):
-            for r in range(1 + h * per_head, min(seq_size, 1 + (h + 1) * per_head)):
-
-                @pl.when(u + 1 < users)
-                def _(r=r):
-                    q_round(u + 1, r)
-
             pair = slice(h // 2 * LANES, h // 2 * LANES + LANES)
             half = (lane // HD) == (h % 2)
             q_head = jnp.where(half, q_user[:, pair] * (HD ** -0.5), 0.0).astype(jnp.bfloat16)
-            q_wide = jnp.concatenate([q_head, mask[u]], axis=1)
+            q_wide = jnp.concatenate([q_head, mask[...]], axis=1)
             best = jnp.full((cands, LANES), 2 * FAR, jnp.float32)
             for e in range(0, events, CHUNK):
                 k_wide = jnp.concatenate(
@@ -309,12 +281,18 @@
                 joined_pair = jnp.where(lane < HD, outs[h - 1], outs[h]).astype(jnp.bfloat16)
                 o_send[u, :, pair] = joined_pair
         lse = peak_all + jnp.log(sum_all)
-        lse_send[u] = lse.T[:8]
-        lse_recv[u, me] = lse_send[u]
+        turned = lse.T[:8]
+        for c in range(cands // LANES):
+            lse_send[u, c] = turned[:, c * LANES : (c + 1) * LANES]
+        lse_recv[u, me] = lse_send[u, me * rows // LANES]
         o_recv[u, me] = o_send[u, row_range(me), :]
         for j in range(1, seq_size):
             o_copy(u, j).start()
             l_copy(u, j).start()
+
+        @pl.when(u + 1 < users)
+        def _():
+            prepare(u + 1)
 
     def combine(u):
         for j in range(1, seq_size):
@@ -323,7 +301,7 @@
         flat = jnp.concatenate([lse_recv[u, s] for s in range(seq_size)], axis=0)
         flat = jnp.pad(flat, ((0, -flat.shape[0] % LANES), (0, 0)))
         lse_turn[...] = flat.T
-        mine = lse_turn[row_range(me), :]
+        mine = lse_turn[pl.ds(pl.multiple_of(lax.rem(me * rows, LANES), rows), rows), :]
         first = lax.broadcasted_iota(jnp.int32, (rows, LANES), 1) < HD
         attended = []
         for h in range(0, heads, 2):
@@ -359,22 +337,24 @@
             total = total + p_recv[u, j].astype(jnp.float32)
         out_ref[u] = total.astype(jnp.bfloat16)
 
+    w_copy.wait()
+
     def stage(t, carry):
         @pl.when(t < users)
         def _():
             attend(t)
 
-        @pl.when((t >= 1) & (t <= users))
+        @pl.when((t >= 2) & (t <= users + 1))
         def _():
-            combine(t - 1)
-
-        @pl.when(t >= 2)
+            combine(t - 2)
+
+        @pl.when(t >= 3)
         def _():
-            finish(t - 2)
+            finish(t - 3)
 
         return carry
 
-    lax.fori_loop(0, users + 2, stage, 0)
+    lax.fori_loop(0, users + 3, stage, 0)
 
     @each_user
     def _(u):
@@ -383,52 +363,47 @@
             l_copy(u, j).wait_send()
         for j in range(1, head_size):
             p_copy(u, j).wait_send()
-        for s in range(seq_size):
-
-            @pl.when((me < seq_size - 1) & (s <= me))
-            def _(s=s):
-                q_copy(u, s, 0).wait_send()
-
-            @pl.when((me > 0) & (s >= me))
-            def _(s=s):
-                q_copy(u, s, 1).wait_send()
+        for j in range(1, seq_size):
+            q_copy(u, j).wait_send()
 
 
 def body(queries, keys, values, hist_len, block_ids, block_count, out_weight):
     users, rows, width = queries.shape
     events = keys.shape[1]
-    slots = block_ids.shape[3]
     seq_size = lax.axis_size("seq")
     head_size = lax.axis_size("heads")
     cands = block_ids.shape[1]
-    if rows % 16 or width % LANES or events % CHUNK or 8 * seq_size > LANES:
+    if users < 2 or seq_size < 3 or rows % 16 or LANES % rows or width % LANES or events % CHUNK or 8 * seq_size > LANES:
         return ring_body(queries, keys, values, hist_len, block_ids, block_count, out_weight)
     vmem = pl.BlockSpec(memory_space=pltpu.VMEM)
-    hbm = pl.BlockSpec(memory_space=pl.ANY)
+    hbm = pl.BlockSpec(memory_space=pltpu.HBM)
     bf16, f32 = jnp.bfloat16, jnp.float32
     dma = pltpu.SemaphoreType.DMA
     return pl.pallas_call(
         functools.partial(kernel, seq_size, head_size),
         out_shape=jax.ShapeDtypeStruct(queries.shape, bf16),
-        in_specs=[vmem, hbm, hbm, vmem, vmem, pl.BlockSpec(memory_space=pltpu.SMEM), vmem],
+        in_specs=[hbm, hbm, hbm, vmem, vmem, pl.BlockSpec(memory_space=pltpu.SMEM), hbm],
         out_specs=vmem,
         scratch_shapes=[
             pltpu.VMEM((users, cands, width), bf16),
+            pltpu.VMEM(out_weight.shape, bf16),
             pltpu.VMEM((users, events, width), bf16),
             pltpu.VMEM((users, events, width), bf16),
-            pltpu.VMEM((users, cands, LANES), bf16),
+            pltpu.VMEM((cands, LANES), bf16),
             pltpu.VMEM((events, LANES), bf16),
             pltpu.VMEM((2, cands, events), f32),
-            pltpu.VMEM((users, 8, cands), f32),
-            pltpu.VMEM((users, seq_size, 8, cands), f32),
-            pltpu.VMEM((cands, LANES), f32),
+            pltpu.VMEM((users, cands // LANES, 8, LANES), f32),
+            pltpu.VMEM((users, seq_size, 8, LANES), f32),
+            pltpu.VMEM((LANES, LANES), f32),
             pltpu.VMEM((users, cands, width), bf16),
             pltpu.VMEM((users, seq_size, rows, width), bf16),
             pltpu.VMEM((users, rows, width), f32),
             pltpu.VMEM((users, head_size, rows, width), bf16),
             pltpu.VMEM((users, head_size, rows, width), bf16),
             dma((users, 2)),
-            dma((users, 2, seq_size)),
+            dma((users,)),
+            dma,
+            dma((users, seq_size)),
             dma((users, seq_size)),
             dma((users, seq_size)),
             dma((users, seq_size)),
@@ -438,11 +413,11 @@
             dma((users, head_size)),
         ],
         compiler_params=pltpu.CompilerParams(
-            collective_id=0, has_side_effects=True, vmem_limit_bytes=48 * 1024 * 1024
+            collective_id=0, has_side_effects=True, vmem_limit_bytes=60 * 1024 * 1024
         ),
     )(
-        queries, keys, values, block_ids.reshape(users, cands, slots),
-        block_count.reshape(users, cands, 1), hist_len, out_weight,
+        queries, keys, values, jnp.swapaxes(block_ids[:, :, 0, :], 1, 2),
+        jnp.swapaxes(block_count, 1, 2), hist_len, out_weight,
     )
 
 

time: 58.4 us -> 41.6 us (0.71)
  Pallas kernels: 50.9 us -> 39.8 us
  local copies, waits for them, and re-layouts: 7.21 us -> 1.57 us
    pallas_call x1, Pallas kernels: 50.9 us -> 39.8 us  [body(): pl.pallas_call(functools.partial(kernel, seq_size, head_size), out_shape=...]
    unnamed x11 -> x1, local copies, waits for them, and re-layouts: 7.21 us -> 1.57 us
where the time goes in v2:
time: 41.6 us; the launch traced here: 41.4 us
  Pallas kernels  39.8 us (96%)
  local copies, waits for them, and re-layouts  1.57 us (4%)
    pallas_call x1, Pallas kernels, body(): pl.pallas_call(functools.partial(kernel, seq_size, head_size), out_shape=...  39.8 us
    unnamed x1, local copies, waits for them, and re-layouts  1.57 us

profile of v2, /device:TPU:0, one launch (start us, length us, event | category | flops | bytes accessed | tf_op | source)
XLA Modules:
  0.0 41.4 jit_solution(16964499571155247127)
XLA Ops:
  0.0 39.8 %shard_map.73 = bf16[4,64,256]{2,1,0:T(8,128)(2,1)} custom-call(bf16[4,64,256]{2,1,0:T(8,128)(2,1)} %q_hbm.1, bf16[4,2048,256]{2,1,0:T(8,128)(2,1)} %k_hbm.1, bf16[4,2048,256]{2,1,0:T(8,128)(2,1)} %v_hbm.1, s32[4,8,256]{2,1,0:T(8,128)} %bitcast.4, s32[4,1,256]{2,1,0:T(1,128)} %bitcast.5, s32[4]{0:T(128)} %length_ref.1, bf16[256,512]{1,0:T(8,128)(2,1)} %w_hbm.1), custom_call_target="tpu_custom_call" | custom-call | tf_op jit(solution)/shard_map/pallas_call | solution.py:382
  39.8 1.6 %copy.9 = bf16[4,64,256]{2,1,0:T(8,128)(2,1)} copy(bf16[4,64,256]{2,1,0:T(8,128)(2,1)} %shard_map.73) | data formatting | bytes 262144

commit v3 on v2

--- a/solution.py
+++ b/solution.py
@@ -344,17 +344,17 @@
         def _():
             attend(t)
 
-        @pl.when((t >= 2) & (t <= users + 1))
+        @pl.when((t >= 3) & (t < users + 3))
         def _():
-            combine(t - 2)
-
-        @pl.when(t >= 3)
+            combine(t - 3)
+
+        @pl.when(t >= 4)
         def _():
-            finish(t - 3)
+            finish(t - 4)
 
         return carry
 
-    lax.fori_loop(0, users + 3, stage, 0)
+    lax.fori_loop(0, users + 4, stage, 0)
 
     @each_user
     def _(u):

time: 41.6 us -> 39.3 us (0.945)
  Pallas kernels: 39.8 us -> 37.5 us
    pallas_call x1, Pallas kernels: 39.8 us -> 37.5 us  [body(): pl.pallas_call(functools.partial(kernel, seq_size, head_size), out_shape=...]
where the time goes in v3:
time: 39.3 us; the launch traced here: 39.1 us
  Pallas kernels  37.5 us (95%)
  local copies, waits for them, and re-layouts  1.57 us (4%)
    pallas_call x1, Pallas kernels, body(): pl.pallas_call(functools.partial(kernel, seq_size, head_size), out_shape=...  37.5 us
    unnamed x1, local copies, waits for them, and re-layouts  1.57 us

profile of v3, /device:TPU:0, one launch (start us, length us, event | category | flops | bytes accessed | tf_op | source)
XLA Modules:
  0.0 39.1 jit_solution(16387685496079474794)
XLA Ops:
  0.0 37.5 %shard_map.73 = bf16[4,64,256]{2,1,0:T(8,128)(2,1)} custom-call(bf16[4,64,256]{2,1,0:T(8,128)(2,1)} %q_hbm.1, bf16[4,2048,256]{2,1,0:T(8,128)(2,1)} %k_hbm.1, bf16[4,2048,256]{2,1,0:T(8,128)(2,1)} %v_hbm.1, s32[4,8,256]{2,1,0:T(8,128)} %bitcast.4, s32[4,1,256]{2,1,0:T(1,128)} %bitcast.5, s32[4]{0:T(128)} %length_ref.1, bf16[256,512]{1,0:T(8,128)(2,1)} %w_hbm.1), custom_call_target="tpu_custom_call" | custom-call | tf_op jit(solution)/shard_map/pallas_call | solution.py:382
  37.5 1.6 %copy.9 = bf16[4,64,256]{2,1,0:T(8,128)(2,1)} copy(bf16[4,64,256]{2,1,0:T(8,128)(2,1)} %shard_map.73) | data formatting | bytes 262144
